TPU v7x, 128 devices: a whole 4x4x4 slice. The times are simulated.
128 devices in a mesh: ctx: 16 (over z, y_hi, core), exp: 8 (over x, y_lo).
Axes of the slice: x: 4, y: 4 (y_hi: 2, y_lo: 2; y = y_hi * 2 + y_lo), z: 4, core: 2. Of those that a mesh axis runs over, the one named last changes fastest.
Arguments:
- tokens: bfloat16 [16384, 2048], P(('ctx', 'exp')), may hold values from -12 to 12
- ln1_gain: float32 [2048], replicated, may hold values from 0.5 to 2
- w_query: bfloat16 [2048, 2048], P(None, 'exp')
- key_weight: bfloat16 [2048, 256], replicated
- value_weight: bfloat16 [2048, 256], replicated, may hold values from -0.125 to 0.125
- q_gain: float32 [128], replicated, may hold values from 0.5 to 5.5
- k_gain: float32 [128], replicated, may hold values from 0.5 to 5.5
- w_out: bfloat16 [2048, 2048], P('exp'), may hold values from -0.125 to 0.125
- ln2_gain: float32 [2048], replicated, may hold values from 0.5 to 2
- expert_ids: int32 [16384, 8], P(('ctx', 'exp')), may hold values from 0 to 127, all different within a row; in each aligned block of 128 rows (0 to 127, 128 to 255, ...) at most 12 rows name the same one
- route_weights: int32 [16384, 8], P(('ctx', 'exp')), may hold values from 1 to 255
- w_gate: bfloat16 [128, 2048, 768], P(('ctx', 'exp')), may hold values from -0.125 to 0.125
- w_up: bfloat16 [128, 2048, 768], P(('ctx', 'exp')), may hold values from -0.125 to 0.125
- w_down: bfloat16 [128, 768, 2048], P(('ctx', 'exp')), may hold values from -0.21875 to 0.21875
Outputs:
- layer_out: bfloat16 [16384, 2048], P(('ctx', 'exp'))
Inputs may be any that keep to these rules, and one draw needn't show every extreme that they name: `expert_ids`: each token names 8 different experts; among the 128 rows of one device no expert is named by more than 12 rows. `route_weights`: a choice weighs the value divided by 1024.
All inputs are finite; a program needn't handle non-finite values.
Results may differ from a plain program's by a relative error of at most 0.02.
The roundings to bfloat16 on the way count: a program that leaves them out, or rounds other values in their place, can miss the bound.
Values may be sent and summed in bfloat16 or wider, within the bound.
A program may use at most 128 MiB of HBM per device.

v0:
```python
import jax
import jax.numpy as jnp
from jax import lax
from jax.sharding import PartitionSpec as P

HEAD_SIZE = 128
QUERY_HEADS = 16
KEY_VALUE_HEADS = 2
TOP = 8
eps_value = 1e-06
theta_value = 1000000.0
floor_value = -1e30
block_span = 1024


def rms_scale(value_states, norm_gain):
    return (
        value_states
        * lax.rsqrt(jnp.mean(value_states * value_states, axis=-1, keepdims=True) + eps_value)
        * norm_gain
    )


def rotate(value_states, positions):
    half_size = value_states.shape[-1] // 2
    frequency = theta_value ** (
        -2.0 * jnp.arange(half_size, dtype=jnp.float32) / value_states.shape[-1]
    )
    angles = positions.astype(jnp.float32)[:, None] * frequency[None, :]
    cosine = jnp.cos(angles)
    sine_part = jnp.sin(angles)
    leading = value_states[..., :half_size]
    second = value_states[..., half_size:]
    return jnp.concatenate(
        [leading * cosine - second * sine_part, second * cosine + leading * sine_part], axis=-1
    )


def attend_block(carried, group_queries, group_first, key_rows, value_rows, key_first):
    running_max, running_sum, weighted = carried
    scores = jnp.einsum(
        "hqd,kd->hqk", group_queries, key_rows, preferred_element_type=jnp.float32
    ) * group_queries.shape[-1] ** (-0.5)
    query_pos = group_first + jnp.arange(group_queries.shape[1])
    key_pos = key_first + jnp.arange(key_rows.shape[0])
    visible = key_pos[None, :] <= query_pos[:, None]
    scores = jnp.where(visible[None], scores, -jnp.inf)
    new_max = jnp.maximum(running_max, jnp.max(scores, axis=-1))
    weights = jnp.exp(scores - new_max[..., None])
    rescale = jnp.exp(running_max - new_max)
    running_sum = running_sum * rescale + jnp.sum(weights, axis=-1)
    weighted = weighted * rescale[..., None] + jnp.einsum(
        "hqk,kd->hqd", weights.astype(jnp.bfloat16), value_rows, preferred_element_type=jnp.float32
    )
    return (new_max, running_sum, weighted)


def scan_keys(group_state, group_queries, group_first, key_rows, value_rows, step_rows):
    group_last = group_first + group_queries.shape[1] - 1

    def one_block(block_index, carried):
        key_first = block_index * step_rows
        key_part = lax.dynamic_slice_in_dim(key_rows, block_index * step_rows, step_rows, 0)
        value_part = lax.dynamic_slice_in_dim(value_rows, block_index * step_rows, step_rows, 0)
        return lax.cond(
            key_first > group_last,
            lambda current: current,
            lambda current: attend_block(
                current, group_queries, group_first, key_part, value_part, key_first
            ),
            carried,
        )

    return lax.fori_loop(0, key_rows.shape[0] // step_rows, one_block, group_state)


def shards(
    tokens,
    ln1_gain,
    w_query,
    key_weight,
    value_weight,
    q_gain,
    k_gain,
    w_out,
    ln2_gain,
    expert_ids,
    route_weights,
    w_gate,
    w_up,
    w_down,
):
    rows_dev = tokens.shape[0]
    ctx_count = lax.axis_size("ctx")
    exp_count = lax.axis_size("exp")
    ctx_rows = rows_dev * exp_count
    heads_dev = w_query.shape[1] // HEAD_SIZE
    group_width = QUERY_HEADS // KEY_VALUE_HEADS
    kv_head = lax.axis_index("exp") * heads_dev // group_width
    inputs32 = tokens.astype(jnp.float32)
    normed_input = rms_scale(inputs32, ln1_gain).astype(jnp.bfloat16)
    key_cols = lax.dynamic_slice_in_dim(key_weight, kv_head * HEAD_SIZE, HEAD_SIZE, 1)
    value_cols = lax.dynamic_slice_in_dim(value_weight, kv_head * HEAD_SIZE, HEAD_SIZE, 1)
    joined = jnp.concatenate([w_query, key_cols, value_cols], axis=1)
    projected = jnp.dot(
        lax.all_gather(normed_input, "exp", axis=0, tiled=True),
        joined,
        preferred_element_type=jnp.float32,
    )
    ctx_first = lax.axis_index("ctx") * ctx_rows
    positions = ctx_first + jnp.arange(ctx_rows)
    query_cols = heads_dev * HEAD_SIZE
    query_heads = (
        projected[:, :query_cols].reshape(ctx_rows, heads_dev, HEAD_SIZE).transpose(1, 0, 2)
    )
    queries = rotate(rms_scale(query_heads, q_gain), positions).astype(jnp.bfloat16)
    keys_all = rotate(
        rms_scale(projected[:, query_cols : query_cols + HEAD_SIZE], k_gain), positions
    ).astype(jnp.bfloat16)
    values_all = projected[:, query_cols + HEAD_SIZE :].astype(jnp.bfloat16)
    groups = ((queries, ctx_first),)
    initial = tuple(
        (
            (
                jnp.full((heads_dev, group_queries.shape[1]), floor_value, jnp.float32),
                jnp.zeros((heads_dev, group_queries.shape[1]), jnp.float32),
                jnp.zeros((heads_dev, group_queries.shape[1], HEAD_SIZE), jnp.float32),
            )
            for group_queries, group_first in groups
        )
    )
    key_rows = lax.all_gather(keys_all, "ctx", axis=0, tiled=True)
    value_rows = lax.all_gather(values_all, "ctx", axis=0, tiled=True)
    finals = tuple(
        (
            scan_keys(group_state, group_queries, group_first, key_rows, value_rows, block_span)
            for (group_queries, group_first), group_state in zip(groups, initial)
        )
    )
    outputs = [
        (weighted / running_sum[..., None]).astype(jnp.bfloat16)
        for running_max, running_sum, weighted in finals
    ]
    merged = outputs[0]
    attended = merged.transpose(1, 0, 2).reshape(ctx_rows, query_cols)
    attention = lax.psum_scatter(
        jnp.dot(attended, w_out, preferred_element_type=jnp.float32).astype(jnp.bfloat16),
        "exp",
        scatter_dimension=0,
        tiled=True,
    ).astype(jnp.float32)
    residual = (inputs32 + attention).astype(jnp.bfloat16)
    normed2 = rms_scale(residual.astype(jnp.float32), ln2_gain).astype(jnp.bfloat16)
    experts = ctx_count * exp_count
    capacity = max(2, 3 * rows_dev * TOP // (2 * experts))
    chosen = expert_ids[:, :, None] == jnp.arange(experts)[None, None, :]
    counts = jnp.sum(chosen, axis=1, dtype=jnp.int32)
    rank_table = jnp.cumsum(counts, axis=0, dtype=jnp.int32) - counts
    slot_index = jnp.sum(jnp.where(chosen, rank_table[:, None, :], 0), axis=2)
    slot_hot = slot_index[:, :, None] == jnp.arange(capacity)[None, None, :]
    dispatch = jnp.einsum(
        "tke,tkc->ect",
        chosen.astype(jnp.bfloat16),
        slot_hot.astype(jnp.bfloat16),
        preferred_element_type=jnp.float32,
    ).astype(jnp.bfloat16)
    outgoing = jnp.einsum(
        "ect,td->ecd", dispatch, normed2, preferred_element_type=jnp.float32
    ).astype(jnp.bfloat16)
    weight_frac = route_weights.astype(jnp.float32) / 1024.0
    combine = jnp.einsum(
        "tke,tkc->tec",
        chosen.astype(jnp.float32) * weight_frac[:, :, None],
        slot_hot.astype(jnp.float32),
    ).astype(jnp.bfloat16)
    width = outgoing.shape[2]
    arrived = lax.all_to_all(outgoing, ("ctx", "exp"), split_axis=0, concat_axis=0, tiled=True)
    flat_rows = arrived.reshape(-1, width)
    gate_act = jnp.dot(flat_rows, w_gate[0], preferred_element_type=jnp.float32)
    up_act = jnp.dot(flat_rows, w_up[0], preferred_element_type=jnp.float32)
    hidden = (jax.nn.silu(gate_act) * up_act).astype(jnp.bfloat16)
    produced = jnp.dot(hidden, w_down[0], preferred_element_type=jnp.float32).astype(jnp.bfloat16)
    returned = lax.all_to_all(
        produced.reshape(arrived.shape), ("ctx", "exp"), split_axis=0, concat_axis=0, tiled=True
    )
    mixture = jnp.einsum("tec,ecd->td", combine, returned, preferred_element_type=jnp.float32)
    return (residual.astype(jnp.float32) + mixture).astype(jnp.bfloat16)


def solution(mesh):
    in_specs = (
        P(("ctx", "exp"), None),
        P(),
        P(None, "exp"),
        P(),
        P(),
        P(),
        P(),
        P("exp", None),
        P(),
        P(("ctx", "exp"), None),
        P(("ctx", "exp"), None),
        P(("ctx", "exp"), None, None),
        P(("ctx", "exp"), None, None),
        P(("ctx", "exp"), None, None),
    )
    out_specs = P(("ctx", "exp"), None)
    return jax.shard_map(shards, mesh=mesh, in_specs=in_specs, out_specs=out_specs, check_vma=False)
```

profile of v0, /device:TPU:42, one launch (start us, length us, event | category | flops | bytes accessed | tf_op | source)
XLA Modules:
  0.0 804.0 jit_solution(13334901165268081912)
XLA Ops:
  7.9 2.0 fusion.42
  10.1 2.2 constant_dynamic-slice_fusion
  12.3 90.0 %all-gather.4.cloned.1.call-done = bf16[1024,2048]{1,0:T(8,128)(2,1)} async-done(((bf16[128,2048]{1,0:T(8,128)(2,1)}), bf16[1024,2048]{1,0:T(8,128)(2,1)}) %all-gather.4.cloned.1.call-update) | async-done | bytes 4194320 | tf_op jit(solution)/shard_map/all_gather | solution.py:106
  102.3 5.2 fusion.33
  113.4 2.3 slice.32
  115.8 2.5 copy.36
  127.2 39.6 %all-gather.6.cloned.1.call-done = bf16[16384,128]{0,1:T(8,128)(2,1)} async-done(((bf16[1024,128]{0,1:T(8,128)(2,1)}), bf16[16384,128]{0,1:T(8,128)(2,1)}) %all-gather.6.cloned.1.call-update) | async-done | bytes 4194320 | tf_op jit(solution)/shard_map/all_gather | solution.py:132
  166.8 6.6 copy.39
  173.5 49.0 %all-gather.8.cloned.1.call-done = bf16[16384,128]{0,1:T(8,128)(2,1)} async-done(((bf16[1024,128]{0,1:T(8,128)(2,1)}), bf16[16384,128]{0,1:T(8,128)(2,1)}) %all-gather.8.cloned.1.call-update) | async-done | bytes 4194320 | tf_op jit(solution)/shard_map/all_gather | solution.py:133
  222.5 6.4 copy.40
  230.0 58.9 %while.17 = (s32[]{:T(128)}, f32[2,1024]{1,0:T(2,128)S(1)}, f32[2,1024]{1,0:T(2,128)S(1)}, f32[2,1024,128]{2,1,0:T(8,128)}, s32[]{:T(128)}, /*index=5*/s32[]{:T(...) while((s32[]{:T(128)}, f32[2,1024]{1,0:T(2,128)S(1)}, ...), condition=%wide.region_8.9_spmd, body=%wide.region_3.8_spmd.sunk | while | flops 1098389504 | bytes 45236608 | solution.py:74
  230.0 11.6 %conditional.2 = (f32[2,1024]{1,0:T(2,128)S(1)}, f32[2,1024]{1,0:T(2,128)S(1)}, f32[2,1024,128]{2,1,0:T(8,128)}) conditional(s32[]{:T(128)} %convert_element_type.167, (s32[]{:T(128)}, s32[]{:T(128)}, bf16[16384,128]{1,0:T(8,128)(2,1)}, bf16[2,1024,128]{2,1,0:T(8,128)(2,1)}, f32[2,1024]{1,0:T(2,128)S(1)}, /*index=5*/f32[2,1024]{1,0:T(2,128)S(1)}, ...), branch_computations={%region_4.6_spmd, %region_7.7_spmd} | conditional | flops 1098389504 | bytes 45219996 | solution.py:65
  231.7 3.3 fusion.2
  235.0 2.0 fusion.1
  237.0 3.6 fusion.6
  241.7 11.6 %conditional.2 = (f32[2,1024]{1,0:T(2,128)S(1)}, f32[2,1024]{1,0:T(2,128)S(1)}, f32[2,1024,128]{2,1,0:T(8,128)}) conditional(s32[]{:T(128)} %convert_element_type.167, (s32[]{:T(128)}, s32[]{:T(128)}, bf16[16384,128]{1,0:T(8,128)(2,1)}, bf16[2,1024,128]{2,1,0:T(8,128)(2,1)}, f32[2,1024]{1,0:T(2,128)S(1)}, /*index=5*/f32[2,1024]{1,0:T(2,128)S(1)}, ...), branch_computations={%region_4.6_spmd, %region_7.7_spmd} | conditional | flops 1098389504 | bytes 45219996 | solution.py:65
  243.3 3.3 fusion.2
  246.6 2.0 fusion.1
  248.6 3.6 fusion.6
  253.3 11.6 %conditional.2 = (f32[2,1024]{1,0:T(2,128)S(1)}, f32[2,1024]{1,0:T(2,128)S(1)}, f32[2,1024,128]{2,1,0:T(8,128)}) conditional(s32[]{:T(128)} %convert_element_type.167, (s32[]{:T(128)}, s32[]{:T(128)}, bf16[16384,128]{1,0:T(8,128)(2,1)}, bf16[2,1024,128]{2,1,0:T(8,128)(2,1)}, f32[2,1024]{1,0:T(2,128)S(1)}, /*index=5*/f32[2,1024]{1,0:T(2,128)S(1)}, ...), branch_computations={%region_4.6_spmd, %region_7.7_spmd} | conditional | flops 1098389504 | bytes 45219996 | solution.py:65
  254.9 3.3 fusion.2
  258.3 2.0 fusion.1
  260.3 3.6 fusion.6
  264.9 11.6 %conditional.2 = (f32[2,1024]{1,0:T(2,128)S(1)}, f32[2,1024]{1,0:T(2,128)S(1)}, f32[2,1024,128]{2,1,0:T(8,128)}) conditional(s32[]{:T(128)} %convert_element_type.167, (s32[]{:T(128)}, s32[]{:T(128)}, bf16[16384,128]{1,0:T(8,128)(2,1)}, bf16[2,1024,128]{2,1,0:T(8,128)(2,1)}, f32[2,1024]{1,0:T(2,128)S(1)}, /*index=5*/f32[2,1024]{1,0:T(2,128)S(1)}, ...), branch_computations={%region_4.6_spmd, %region_7.7_spmd} | conditional | flops 1098389504 | bytes 45219996 | solution.py:65
  266.6 3.3 fusion.2
  269.9 2.0 fusion.1
  271.9 3.6 fusion.6
  276.6 11.6 %conditional.2 = (f32[2,1024]{1,0:T(2,128)S(1)}, f32[2,1024]{1,0:T(2,128)S(1)}, f32[2,1024,128]{2,1,0:T(8,128)}) conditional(s32[]{:T(128)} %convert_element_type.167, (s32[]{:T(128)}, s32[]{:T(128)}, bf16[16384,128]{1,0:T(8,128)(2,1)}, bf16[2,1024,128]{2,1,0:T(8,128)(2,1)}, f32[2,1024]{1,0:T(2,128)S(1)}, /*index=5*/f32[2,1024]{1,0:T(2,128)S(1)}, ...), branch_computations={%region_4.6_spmd, %region_7.7_spmd} | conditional | flops 1098389504 | bytes 45219996 | solution.py:65
  278.2 3.3 fusion.2
  281.6 2.0 fusion.1
  283.6 3.6 fusion.6
  288.9 2.5 copy.41
  292.8 4.5 convolution_convert_fusion.2
  297.8 2.4 select_reduce_fusion
  300.2 2.3 fusion.39
  302.5 211.1 %reduce-scatter.2.cloned.1.call-done = bf16[128,2048]{1,0:T(8,128)(2,1)} async-done(((bf16[1024,2048]{1,0:T(8,128)(2,1)}), bf16[128,2048]{1,0:T(8,128)(2,1)}) %reduce-scatter.2.cloned.1.call-update) | async-done | bytes 524304 | tf_op jit(solution)/shard_map/reduce_scatter | solution.py:146
  515.1 3.2 convolution_convert_fusion.1
  518.4 6.9 copy.45
  525.2 104.3 %all_to_all.10 = bf16[128,12,2048]{2,1,0:T(8,128)(2,1)} all-to-all(bf16[128,12,2048]{2,1,0:T(8,128)(2,1)} %copy.45), channel_id=1, replica_groups=mesh['ctx'=16,'exp'=8] {'ctx','exp'}, dimensions={0} | all-to-all | bytes 12582912 | tf_op jit(solution)/shard_map/all_to_all | solution.py:177
  629.5 10.7 %reshape.167 = bf16[1536,2048]{1,0:T(8,128)(2,1)} reshape(bf16[128,12,2048]{2,1,0:T(8,128)(2,1)} %all_to_all.10) | data formatting | bytes 12582912 | tf_op jit(solution)/shard_map/reshape | solution.py:178
  640.2 8.2 %fusion.22 = f32[1536,768]{1,0:T(8,128)S(1)} fusion(bf16[1536,2048]{1,0:T(8,128)(2,1)} %reshape.167, bf16[1,2048,768]{2,1,0:T(8,128)(2,1)} %param.29), kind=kOutput, calls=%fused_computation.30 | convolution fusion | flops 4831838208 | bytes 14155776 | tf_op jit(solution)/shard_map/dot_general | solution.py:179
  648.4 5.6 multiply_convert_fusion
  654.0 7.1 convolution_convert_fusion
  661.1 10.6 %reshape.168 = bf16[128,12,2048]{2,1,0:T(8,128)(2,1)} reshape(bf16[1536,2048]{1,0:T(8,128)(2,1)} %convolution_convert_fusion) | data formatting | bytes 12582912 | tf_op jit(solution)/shard_map/reshape | solution.py:184
  671.7 10.3 %all-to-all-start.1 = ((bf16[128,12,2048]{2,1,0:T(8,128)(2,1)}), bf16[128,12,2048]{2,1,0:T(8,128)(2,1)}, u32[]{:S(2)}, u32[]{:S(2)}) async-start(bf16[128,12,2048]{2,1,0:T(8,128)(2,1)} %reshape.168), calls=%async_computation.2 | async-start | bytes 16777216 | tf_op jit(solution)/shard_map/all_to_all | solution.py:183
  682.2 2.0 convolution_convert_fusion.3
  684.1 101.5 %all-to-all-done.1 = bf16[128,12,2048]{2,1,0:T(8,128)(2,1)} async-done(((bf16[128,12,2048]{2,1,0:T(8,128)(2,1)}), bf16[128,12,2048]{2,1,0:T(8,128)(2,1)}, u32[]{:S(2)}, u32[]{:S(2)}) %all-to-all-start.1) | async-done | bytes 6291488 | tf_op jit(solution)/shard_map/all_to_all | solution.py:183
  785.6 11.6 %fusion.30 = bf16[128,2048]{1,0:T(8,128)(2,1)} fusion(bf16[128,12,2048]{2,1,0:T(8,128)(2,1)} %all-to-all-done.1, bf16[128,128,12]{1,2,0:T(8,128)(2,1)} %convolution_convert_fusion.3, bf16[128,2048]{1,0:T(8,128)(2,1)} %reduce-scatter.2.cloned.1.call-done, bf16[128,2048]{1,0:T(8,128)(2,1)} %param.18), kind=kOutput, calls=%fused_computation.34 | convolution fusion | flops 807141376 | bytes 8257536 | tf_op jit(solution)/shard_map/tec,ecd->td/dot_general | solution.py:186
  (143 shorter events, 34.7 us)
Async XLA Ops:
  6.5 647.5 %copy-start = (bf16[1,768,2048]{2,1,0:T(8,128)(2,1)S(1)}, bf16[1,768,2048]{2,1,0:T(8,128)(2,1)}, u32[]{:S(2)}) copy-start(bf16[1,768,2048]{2,1,0:T(8,128)(2,1)} %param.31) | copy-start | bytes 9437188
  6.5 95.8 %all-gather.4.cloned.1.call-start = ((), (), s32[]{:S(2)}) async-start(), calls=%async_computation.3 | async-start | bytes 4718592 | tf_op jit(solution)/shard_map/all_gather | solution.py:106
  10.0 156.8 %all-gather.6.cloned.1.call-start = ((), (), s32[]{:S(2)}) async-start(), calls=%async_computation.4 | async-start | bytes 4456448 | tf_op jit(solution)/shard_map/all_gather | solution.py:132
  102.3 6.6 copy-start.9
  107.5 1.4 copy-start.5
  109.0 13.9 %copy-start.10 = (f32[128]{0:T(128)S(1)}, f32[128]{0:T(128)}, u32[]{:S(2)}) copy-start(f32[128]{0:T(128)} %param.23) | copy-start | bytes 1540
  111.5 111.0 %all-gather.8.cloned.1.call-start = ((), (), s32[]{:S(2)}) async-start(), calls=%async_computation.5 | async-start | bytes 4456448 | tf_op jit(solution)/shard_map/all_gather | solution.py:133
  113.4 400.2 %reduce-scatter.2.cloned.1.call-start = ((), (), s32[]{:S(2)}) async-start(), calls=%async_computation.6 | async-start | bytes 4718592 | tf_op jit(solution)/shard_map/reduce_scatter | solution.py:146
  231.7 3.3 copy-start.1
  235.0 2.0 copy-start.3
  240.6 1.1 copy-start.4
  243.3 3.3 copy-start.1
  246.6 2.0 copy-start.3
  252.2 1.1 copy-start.4
  254.9 3.3 copy-start.1
  258.3 2.0 copy-start.3
  263.9 1.1 copy-start.4
  266.6 3.3 copy-start.1
  269.9 2.0 copy-start.3
  275.5 1.1 copy-start.4
  278.2 3.3 copy-start.1
  281.5 2.0 copy-start.3
  287.2 1.1 copy-start.4
  292.8 4.5 copy-start.7
  297.3 217.8 %copy-start.6 = (f32[2048]{0:T(1024)S(1)}, f32[2048]{0:T(1024)}, u32[]{:S(2)}) copy-start(f32[2048]{0:T(1024)} %param.26) | copy-start | bytes 24580
  640.2 8.2 %copy-start.2 = (bf16[1536,2048]{1,0:T(8,128)(2,1)S(1)}, bf16[1536,2048]{1,0:T(8,128)(2,1)}, u32[]{:S(2)}) copy-start(bf16[1536,2048]{1,0:T(8,128)(2,1)} %reshape.167) | copy-start | bytes 18874372
  640.2 8.2 %copy-start.11 = (bf16[1,2048,768]{2,1,0:T(8,128)(2,1)S(1)}, bf16[1,2048,768]{2,1,0:T(8,128)(2,1)}, u32[]{:S(2)}) copy-start(bf16[1,2048,768]{2,1,0:T(8,128)(2,1)} %param.30) | copy-start | bytes 9437188
  671.7 10.3 %copy-start.8 = (s32[128,8]{0,1:T(8,128)S(1)}, s32[128,8]{0,1:T(8,128)}, u32[]{:S(2)}) copy-start(s32[128,8]{0,1:T(8,128)} %param.28) | copy-start | bytes 12292
  671.7 113.9 %all-to-all-start.1 = ((bf16[128,12,2048]{2,1,0:T(8,128)(2,1)}), bf16[128,12,2048]{2,1,0:T(8,128)(2,1)}, u32[]{:S(2)}, u32[]{:S(2)}) async-start(bf16[128,12,2048]{2,1,0:T(8,128)(2,1)} %reshape.168), calls=%async_computation.2 | async-start | bytes 16777216 | tf_op jit(solution)/shard_map/all_to_all | solution.py:183
Sparse Core Ops, SparseCore 0:
  10.1 92.1 all-gather.3
  111.7 55.1 all-gather.5
  169.3 53.1 all-gather.7
  297.4 216.1 reduce-scatter.1
where the time goes:
time: 811 us; the launch traced here: 804 us
  waiting for transfers between devices  491 us (61%)
  blocking collectives  104 us (13%)
  matrix products  84.1 us (10%)
  local copies, waits for them, and re-layouts  63.6 us (8%)
  other arithmetic  35.8 us (4%)
  between operations  13.6 us (2%)
  starting transfers between devices  10.4 us (1%)
    reduce_scatter x1, waiting for transfers between devices, shards(): lax.psum_scatter(jnp.dot(attended, w_out, preferred_element_type=jnp.floa...  211 us
    all_to_all x1, blocking collectives, shards(): lax.all_to_all(outgoing, ('ctx', 'exp'), split_axis=0, concat_axis=0, til...  104 us
    all_to_all x1, waiting for transfers between devices, shards(): lax.all_to_all(produced.reshape(arrived.shape), ('ctx', 'exp'), split_axi...  101 us
    all_gather x1, waiting for transfers between devices, shards(): lax.all_gather(normed_input, 'exp', axis=0, tiled=True)  90 us
    all_gather x1, waiting for transfers between devices, shards(): value_rows = lax.all_gather(values_all, 'ctx', axis=0, tiled=True)  49 us
    all_gather x1, waiting for transfers between devices, shards(): key_rows = lax.all_gather(keys_all, 'ctx', axis=0, tiled=True)  39.6 us
    dot_general x5, matrix products, attend_block(): jnp.einsum('hqk,kd->hqd', weights.astype(jnp.bfloat16), value_rows, prefe...  17.9 us
    dot_general x5, matrix products, attend_block(): jnp.einsum('hqd,kd->hqk', group_queries, key_rows, preferred_element_type...  16.5 us
  transfers between devices with their start and end apart: 5, of which 5 were waited for; matrix products, arithmetic and copies ran while one was open for 4% of the time, Pallas kernels for 0%

commit v1 on v0

--- a/solution.py
+++ b/solution.py
@@ -129,8 +129,17 @@
             for group_queries, group_first in groups
         )
     )
-    key_rows = lax.all_gather(keys_all, "ctx", axis=0, tiled=True)
-    value_rows = lax.all_gather(values_all, "ctx", axis=0, tiled=True)
+
+    def launch_goods_now(incoming_x, sample):
+        return jnp.split(
+            lax.all_gather(
+                jnp.concatenate([sample, incoming_x], axis=1), axis=0, axis_name="ctx", tiled=True
+            ),
+            [sample.shape[1]],
+            axis=1,
+        )
+
+    key_rows, value_rows = launch_goods_now(values_all, keys_all)
     finals = tuple(
         (
             scan_keys(group_state, group_queries, group_first, key_rows, value_rows, block_span)

time: 811 us -> 784 us (0.967)
  waiting for transfers between devices: 491 us -> 461 us
    all_gather x2 -> x1, waiting for transfers between devices: 88.6 us -> 59 us  [launch_goods_now(): lax.all_gather(jnp.concatenate([sample, incoming_x], axis=1), axis=0, axi...]
  transfers between devices with their start and end apart: 5 -> 4, of which waited for: 5 -> 4; matrix products, arithmetic and copies ran while one was open for 4% -> 3% of each run, Pallas kernels for 0% -> 0%
where the time goes in v1:
time: 784 us; the launch traced here: 778 us
  waiting for transfers between devices  461 us (59%)
  blocking collectives  104 us (13%)
  matrix products  84.1 us (11%)
  local copies, waits for them, and re-layouts  67.5 us (9%)
  other arithmetic  35.8 us (5%)
  between operations  13.6 us (2%)
  starting transfers between devices  10.4 us (1%)
    reduce_scatter x1, waiting for transfers between devices, shards(): lax.psum_scatter(jnp.dot(attended, w_out, preferred_element_type=jnp.floa...  210 us
    all_to_all x1, blocking collectives, shards(): lax.all_to_all(outgoing, ('ctx', 'exp'), split_axis=0, concat_axis=0, til...  104 us
    all_to_all x1, waiting for transfers between devices, shards(): lax.all_to_all(produced.reshape(arrived.shape), ('ctx', 'exp'), split_axi...  101 us
    all_gather x1, waiting for transfers between devices, shards(): lax.all_gather(normed_input, 'exp', axis=0, tiled=True)  90 us
    all_gather x1, waiting for transfers between devices, launch_goods_now(): lax.all_gather(jnp.concatenate([sample, incoming_x], axis=1), axis=0, axi...  59 us
    dot_general x5, matrix products, attend_block(): jnp.einsum('hqk,kd->hqd', weights.astype(jnp.bfloat16), value_rows, prefe...  18 us
    dot_general x5, matrix products, attend_block(): jnp.einsum('hqd,kd->hqk', group_queries, key_rows, preferred_element_type...  16.5 us
  transfers between devices with their start and end apart: 4, of which 4 were waited for; matrix products, arithmetic and copies ran while one was open for 3% of the time, Pallas kernels for 0%

profile of v1, /device:TPU:42, one launch (start us, length us, event | category | flops | bytes accessed | tf_op | source)
XLA Modules:
  0.0 777.7 jit_solution(4211398964917344859)
XLA Ops:
  7.9 2.0 fusion.42
  10.1 2.3 constant_dynamic-slice_fusion
  12.3 90.0 %all-gather.3.cloned.1.call-done = bf16[1024,2048]{1,0:T(8,128)(2,1)} async-done(((bf16[128,2048]{1,0:T(8,128)(2,1)}), bf16[1024,2048]{1,0:T(8,128)(2,1)}) %all-gather.3.cloned.1.call-update) | async-done | bytes 4194320 | tf_op jit(solution)/shard_map/all_gather | solution.py:106
  102.3 5.2 fusion.33
  111.7 2.3 slice.33
  114.0 2.6 copy.36
  125.5 59.0 %all-gather.5.cloned.1.call-done = bf16[16384,256]{0,1:T(8,128)(2,1)} async-done(((bf16[1024,256]{0,1:T(8,128)(2,1)}), bf16[16384,256]{0,1:T(8,128)(2,1)}) %all-gather.5.cloned.1.call-update) | async-done | bytes 8388624 | tf_op jit(solution)/shard_map/all_gather | solution.py:135
  184.6 6.1 fusion.65
  190.6 6.4 copy.39
  197.0 6.4 copy.40
  204.5 58.8 %while.17 = (s32[]{:T(128)}, f32[2,1024]{1,0:T(2,128)S(1)}, f32[2,1024]{1,0:T(2,128)S(1)}, f32[2,1024,128]{2,1,0:T(8,128)}, s32[]{:T(128)}, /*index=5*/s32[]{:T(...) while((s32[]{:T(128)}, f32[2,1024]{1,0:T(2,128)S(1)}, ...), condition=%wide.region_8.9_spmd, body=%wide.region_3.8_spmd.sunk | while | flops 1098389504 | bytes 45236608 | solution.py:74
  204.5 11.6 %conditional.2 = (f32[2,1024]{1,0:T(2,128)S(1)}, f32[2,1024]{1,0:T(2,128)S(1)}, f32[2,1024,128]{2,1,0:T(8,128)}) conditional(s32[]{:T(128)} %convert_element_type.167, (s32[]{:T(128)}, s32[]{:T(128)}, bf16[16384,128]{1,0:T(8,128)(2,1)}, bf16[2,1024,128]{2,1,0:T(8,128)(2,1)}, f32[2,1024]{1,0:T(2,128)S(1)}, /*index=5*/f32[2,1024]{1,0:T(2,128)S(1)}, ...), branch_computations={%region_4.6_spmd, %region_7.7_spmd} | conditional | flops 1098389504 | bytes 45219996 | solution.py:65
  206.1 3.3 fusion.2
  209.5 2.0 fusion.1
  211.5 3.6 fusion.6
  216.1 11.6 %conditional.2 = (f32[2,1024]{1,0:T(2,128)S(1)}, f32[2,1024]{1,0:T(2,128)S(1)}, f32[2,1024,128]{2,1,0:T(8,128)}) conditional(s32[]{:T(128)} %convert_element_type.167, (s32[]{:T(128)}, s32[]{:T(128)}, bf16[16384,128]{1,0:T(8,128)(2,1)}, bf16[2,1024,128]{2,1,0:T(8,128)(2,1)}, f32[2,1024]{1,0:T(2,128)S(1)}, /*index=5*/f32[2,1024]{1,0:T(2,128)S(1)}, ...), branch_computations={%region_4.6_spmd, %region_7.7_spmd} | conditional | flops 1098389504 | bytes 45219996 | solution.py:65
  217.7 3.3 fusion.2
  221.1 2.0 fusion.1
  223.1 3.6 fusion.6
  227.7 11.6 %conditional.2 = (f32[2,1024]{1,0:T(2,128)S(1)}, f32[2,1024]{1,0:T(2,128)S(1)}, f32[2,1024,128]{2,1,0:T(8,128)}) conditional(s32[]{:T(128)} %convert_element_type.167, (s32[]{:T(128)}, s32[]{:T(128)}, bf16[16384,128]{1,0:T(8,128)(2,1)}, bf16[2,1024,128]{2,1,0:T(8,128)(2,1)}, f32[2,1024]{1,0:T(2,128)S(1)}, /*index=5*/f32[2,1024]{1,0:T(2,128)S(1)}, ...), branch_computations={%region_4.6_spmd, %region_7.7_spmd} | conditional | flops 1098389504 | bytes 45219996 | solution.py:65
  229.4 3.3 fusion.2
  232.7 2.0 fusion.1
  234.7 3.6 fusion.6
  239.4 11.6 %conditional.2 = (f32[2,1024]{1,0:T(2,128)S(1)}, f32[2,1024]{1,0:T(2,128)S(1)}, f32[2,1024,128]{2,1,0:T(8,128)}) conditional(s32[]{:T(128)} %convert_element_type.167, (s32[]{:T(128)}, s32[]{:T(128)}, bf16[16384,128]{1,0:T(8,128)(2,1)}, bf16[2,1024,128]{2,1,0:T(8,128)(2,1)}, f32[2,1024]{1,0:T(2,128)S(1)}, /*index=5*/f32[2,1024]{1,0:T(2,128)S(1)}, ...), branch_computations={%region_4.6_spmd, %region_7.7_spmd} | conditional | flops 1098389504 | bytes 45219996 | solution.py:65
  241.0 3.3 fusion.2
  244.3 2.0 fusion.1
  246.3 3.6 fusion.6
  251.0 11.6 %conditional.2 = (f32[2,1024]{1,0:T(2,128)S(1)}, f32[2,1024]{1,0:T(2,128)S(1)}, f32[2,1024,128]{2,1,0:T(8,128)}) conditional(s32[]{:T(128)} %convert_element_type.167, (s32[]{:T(128)}, s32[]{:T(128)}, bf16[16384,128]{1,0:T(8,128)(2,1)}, bf16[2,1024,128]{2,1,0:T(8,128)(2,1)}, f32[2,1024]{1,0:T(2,128)S(1)}, /*index=5*/f32[2,1024]{1,0:T(2,128)S(1)}, ...), branch_computations={%region_4.6_spmd, %region_7.7_spmd} | conditional | flops 1098389504 | bytes 45219996 | solution.py:65
  252.6 3.3 fusion.2
  255.9 2.0 fusion.1
  257.9 3.6 fusion.6
  263.3 2.5 copy.41
  267.1 4.5 convolution_convert_fusion.2
  272.2 2.4 select_reduce_fusion
  274.6 2.3 fusion.39
  276.9 210.5 %reduce-scatter.2.cloned.1.call-done = bf16[128,2048]{1,0:T(8,128)(2,1)} async-done(((bf16[1024,2048]{1,0:T(8,128)(2,1)}), bf16[128,2048]{1,0:T(8,128)(2,1)}) %reduce-scatter.2.cloned.1.call-update) | async-done | bytes 524304 | tf_op jit(solution)/shard_map/reduce_scatter | solution.py:155
  488.9 3.2 convolution_convert_fusion.1
  492.1 6.8 copy.45
  499.0 104.3 %all_to_all.10 = bf16[128,12,2048]{2,1,0:T(8,128)(2,1)} all-to-all(bf16[128,12,2048]{2,1,0:T(8,128)(2,1)} %copy.45), channel_id=1, replica_groups=mesh['ctx'=16,'exp'=8] {'ctx','exp'}, dimensions={0} | all-to-all | bytes 12582912 | tf_op jit(solution)/shard_map/all_to_all | solution.py:186
  603.3 10.7 %reshape.167 = bf16[1536,2048]{1,0:T(8,128)(2,1)} reshape(bf16[128,12,2048]{2,1,0:T(8,128)(2,1)} %all_to_all.10) | data formatting | bytes 12582912 | tf_op jit(solution)/shard_map/reshape | solution.py:187
  614.0 8.2 %fusion.22 = f32[1536,768]{1,0:T(8,128)S(1)} fusion(bf16[1536,2048]{1,0:T(8,128)(2,1)} %reshape.167, bf16[1,2048,768]{2,1,0:T(8,128)(2,1)} %param.29), kind=kOutput, calls=%fused_computation.30 | convolution fusion | flops 4831838208 | bytes 14155776 | tf_op jit(solution)/shard_map/dot_general | solution.py:188
  622.2 5.6 multiply_convert_fusion
  627.8 7.1 convolution_convert_fusion
  634.9 10.6 %reshape.168 = bf16[128,12,2048]{2,1,0:T(8,128)(2,1)} reshape(bf16[1536,2048]{1,0:T(8,128)(2,1)} %convolution_convert_fusion) | data formatting | bytes 12582912 | tf_op jit(solution)/shard_map/reshape | solution.py:193
  645.5 10.3 %all-to-all-start.1 = ((bf16[128,12,2048]{2,1,0:T(8,128)(2,1)}), bf16[128,12,2048]{2,1,0:T(8,128)(2,1)}, u32[]{:S(2)}, u32[]{:S(2)}) async-start(bf16[128,12,2048]{2,1,0:T(8,128)(2,1)} %reshape.168), calls=%async_computation.2 | async-start | bytes 16777216 | tf_op jit(solution)/shard_map/all_to_all | solution.py:192
  655.9 2.0 convolution_convert_fusion.3
  657.9 101.5 %all-to-all-done.1 = bf16[128,12,2048]{2,1,0:T(8,128)(2,1)} async-done(((bf16[128,12,2048]{2,1,0:T(8,128)(2,1)}), bf16[128,12,2048]{2,1,0:T(8,128)(2,1)}, u32[]{:S(2)}, u32[]{:S(2)}) %all-to-all-start.1) | async-done | bytes 6291488 | tf_op jit(solution)/shard_map/all_to_all | solution.py:192
  759.4 11.6 %fusion.30 = bf16[128,2048]{1,0:T(8,128)(2,1)} fusion(bf16[128,12,2048]{2,1,0:T(8,128)(2,1)} %all-to-all-done.1, bf16[128,128,12]{1,2,0:T(8,128)(2,1)} %convolution_convert_fusion.3, bf16[128,2048]{1,0:T(8,128)(2,1)} %reduce-scatter.2.cloned.1.call-done, bf16[128,2048]{1,0:T(8,128)(2,1)} %param.18), kind=kOutput, calls=%fused_computation.34 | convolution fusion | flops 807141376 | bytes 8257536 | tf_op jit(solution)/shard_map/tec,ecd->td/dot_general | solution.py:195
  (141 shorter events, 32.8 us)
Async XLA Ops:
  6.5 621.3 %copy-start = (bf16[1,768,2048]{2,1,0:T(8,128)(2,1)S(1)}, bf16[1,768,2048]{2,1,0:T(8,128)(2,1)}, u32[]{:S(2)}) copy-start(bf16[1,768,2048]{2,1,0:T(8,128)(2,1)} %param.31) | copy-start | bytes 9437188
  6.5 95.8 %all-gather.3.cloned.1.call-start = ((), (), s32[]{:S(2)}) async-start(), calls=%async_computation.3 | async-start | bytes 4718592 | tf_op jit(solution)/shard_map/all_gather | solution.py:106
  10.0 174.6 %all-gather.5.cloned.1.call-start = ((), (), s32[]{:S(2)}) async-start(), calls=%async_computation.4 | async-start | bytes 8912896 | tf_op jit(solution)/shard_map/all_gather | solution.py:135
  102.3 6.5 copy-start.9
  107.5 1.4 copy-start.5
  109.0 12.2 %copy-start.10 = (f32[128]{0:T(128)S(1)}, f32[128]{0:T(128)}, u32[]{:S(2)}) copy-start(f32[128]{0:T(128)} %param.23) | copy-start | bytes 1540
  111.6 375.8 %reduce-scatter.2.cloned.1.call-start = ((), (), s32[]{:S(2)}) async-start(), calls=%async_computation.5 | async-start | bytes 4718592 | tf_op jit(solution)/shard_map/reduce_scatter | solution.py:155
  206.1 3.3 copy-start.1
  209.5 2.0 copy-start.3
  215.1 1.0 copy-start.4
  217.7 3.3 copy-start.1
  221.1 2.0 copy-start.3
  226.7 1.0 copy-start.4
  229.4 3.3 copy-start.1
  232.7 2.0 copy-start.3
  238.3 1.0 copy-start.4
  241.0 3.3 copy-start.1
  244.3 2.0 copy-start.3
  249.9 1.0 copy-start.4
  252.6 3.3 copy-start.1
  255.9 2.0 copy-start.3
  261.5 1.0 copy-start.4
  267.1 4.5 copy-start.7
  271.6 217.2 %copy-start.6 = (f32[2048]{0:T(1024)S(1)}, f32[2048]{0:T(1024)}, u32[]{:S(2)}) copy-start(f32[2048]{0:T(1024)} %param.26) | copy-start | bytes 24580
  614.0 8.2 %copy-start.2 = (bf16[1536,2048]{1,0:T(8,128)(2,1)S(1)}, bf16[1536,2048]{1,0:T(8,128)(2,1)}, u32[]{:S(2)}) copy-start(bf16[1536,2048]{1,0:T(8,128)(2,1)} %reshape.167) | copy-start | bytes 18874372
  614.0 8.2 %copy-start.11 = (bf16[1,2048,768]{2,1,0:T(8,128)(2,1)S(1)}, bf16[1,2048,768]{2,1,0:T(8,128)(2,1)}, u32[]{:S(2)}) copy-start(bf16[1,2048,768]{2,1,0:T(8,128)(2,1)} %param.30) | copy-start | bytes 9437188
  645.5 10.3 %copy-start.8 = (s32[128,8]{0,1:T(8,128)S(1)}, s32[128,8]{0,1:T(8,128)}, u32[]{:S(2)}) copy-start(s32[128,8]{0,1:T(8,128)} %param.28) | copy-start | bytes 12292
  645.5 113.9 %all-to-all-start.1 = ((bf16[128,12,2048]{2,1,0:T(8,128)(2,1)}), bf16[128,12,2048]{2,1,0:T(8,128)(2,1)}, u32[]{:S(2)}, u32[]{:S(2)}) async-start(bf16[128,12,2048]{2,1,0:T(8,128)(2,1)} %reshape.168), calls=%async_computation.2 | async-start | bytes 16777216 | tf_op jit(solution)/shard_map/all_to_all | solution.py:192
Sparse Core Ops, SparseCore 0:
  10.1 92.1 all-gather.2
  111.8 72.7 all-gather.4
  271.8 215.5 reduce-scatter.1
